TPU v7x, 512 devices: a whole 4x8x8 slice. The times are simulated.
512 devices in a mesh: clip: 32 (over x, y), seq: 16 (over z, core).
Axes of the slice: x: 4, y: 8, z: 8, core: 2. Of those that a mesh axis runs over, the one named last changes fastest.
Arguments:
- queries: bfloat16 [32, 2048, 4096], P('clip', 'seq'), may hold values from -34 to 34
- keys: bfloat16 [32, 2048, 4096], P('clip', 'seq'), may hold values from -6 to 6
- values: bfloat16 [32, 2048, 4096], P('clip', 'seq'), may hold values from -6 to 6
- frame_counts: int32 [128], P('clip'), may hold values from 1 to 4
- assignment: int32 [32], P('clip'), may hold values from 0 to 127
- timesteps: int32 [32], P('clip'), may hold values from 0 to 999
- gate_gain: float32 [4096], replicated, may hold values from -3 to 3
Outputs:
- attended: bfloat16 [32, 2048, 4096], P('clip', 'seq')
All inputs are finite; a program needn't handle non-finite values.
Results may differ from a plain program's by a relative error of at most 0.0086.
Values may be sent and summed in bfloat16 or wider, within the bound.
A program may use at most 128 MiB of HBM per device.

v0:
```python
import jax
import jax.numpy as jnp
from jax import lax
from jax.sharding import Mesh
from jax.sharding import PartitionSpec as P

HD = 128
FRAME_TOK = 448
GRID_W = 28
CLIP = ("clip_0", "clip_1")


def in_order(tiles, dim):
    dims = list(tiles.shape[1:])
    dims[dim] *= tiles.shape[0]
    return jnp.moveaxis(tiles, 0, dim).reshape(dims)


def all_blocks(shard, axes, sequence):
    tiles = shard
    for k in sequence:
        tiles = lax.all_gather(tiles, axes[k])
    done = sequence[::-1]
    back = [done.index(k) for k in range(len(axes))]
    tiles = tiles.transpose(*back, *range(len(axes), tiles.ndim))
    return tiles.reshape(-1, *shard.shape)


def gathered_by_axis(shard, axes, sequence, dim):
    return in_order(all_blocks(shard, axes, sequence), dim)


def sent_together(arrays, axis, split_dim, concat_dim, along):
    both = jnp.concatenate(arrays, axis=along)
    out, at, done = (
        lax.all_to_all(both, axis, split_axis=split_dim, concat_axis=concat_dim, tiled=True),
        0,
        [],
    )
    for a in arrays:
        done.append(lax.slice_in_dim(out, at, at + a.shape[along], axis=along))
        at += a.shape[along]
    return tuple(done)


def rope_tables(count):
    position = jnp.arange(count, dtype=jnp.int32)
    frame = (position // FRAME_TOK).astype(jnp.float32)
    within = position % FRAME_TOK
    row_pos = (within // GRID_W).astype(jnp.float32)
    col_pos = (within % GRID_W).astype(jnp.float32)
    temporal = jnp.arange(22, dtype=jnp.float32)
    spatial = jnp.arange(21, dtype=jnp.float32)
    inv_time = 10000.0 ** (-2.0 * temporal / 44.0)
    inv_space = 10000.0 ** (-2.0 * spatial / 42.0)
    angles = jnp.concatenate(
        [
            frame[:, None] * inv_time[None, :],
            row_pos[:, None] * inv_space[None, :],
            col_pos[:, None] * inv_space[None, :],
        ],
        axis=1,
    )
    return (jnp.cos(angles), jnp.sin(angles))


def rotate(vectors, cosine, sine):
    half = vectors.shape[-1] // 2
    first = vectors[..., :half].astype(jnp.float32)
    second = vectors[..., half:].astype(jnp.float32)
    cos_b = cosine[:, None, :]
    sin_b = sine[:, None, :]
    return jnp.concatenate(
        [first * cos_b - second * sin_b, first * sin_b + second * cos_b], axis=-1
    ).astype(jnp.bfloat16)


def masked_scores(q_block, key_rot, width, length, scale):
    scores = (
        jnp.einsum("qhd,khd->hqk", q_block, key_rot, preferred_element_type=jnp.float32) * scale
    )
    key_pos = jnp.arange(width, dtype=jnp.int32)
    return jnp.where(key_pos[None, None, :] < length, scores, -jnp.inf)


def attend(query_rot, key_rot, value, length):
    count = query_rot.shape[0]
    width = min(512, count)
    scale = HD ** (-0.5)
    results = []
    for start in range(0, count, width):
        q_block = query_rot[start : start + width]
        scores = masked_scores(q_block, key_rot, count, length, scale)
        top = jnp.max(scores, axis=-1, keepdims=True)
        weights = jnp.exp(scores - top)
        total = jnp.sum(weights, axis=-1)
        mixed = jnp.einsum(
            "hqk,khd->qhd", weights.astype(jnp.bfloat16), value, preferred_element_type=jnp.float32
        )
        results.append(mixed / jnp.transpose(total)[:, :, None])
    return jnp.concatenate(results, axis=0).astype(jnp.bfloat16)


def local(queries, keys, values, frame_counts, assignment, timesteps, gate_gain):
    counts_all = gathered_by_axis(frame_counts, CLIP, (0, 1), 0)
    slots = jnp.arange(counts_all.shape[0], dtype=jnp.int32)
    picked = jnp.sum(jnp.where(slots == assignment[0], counts_all, 0))
    length = picked * FRAME_TOK
    fraction = timesteps[0].astype(jnp.float32) / 1000.0
    sigma = 5.0 * fraction / (1.0 + 4.0 * fraction)
    tok_rows = queries.shape[1]
    feature_count = queries.shape[2]
    groups = lax.axis_size("seq")
    heads_local = feature_count // HD // groups
    query_rows = queries.reshape(tok_rows, groups, heads_local, HD)
    key_rows = keys.reshape(tok_rows, groups, heads_local, HD)
    value_rows = values.reshape(tok_rows, groups, heads_local, HD)
    q_heads, k_heads, v_heads = sent_together((query_rows, key_rows, value_rows), "seq", 1, 0, 2)
    count = q_heads.shape[0]
    heads_here = q_heads.shape[2]
    cosine, sine = rope_tables(count)
    query_rot = rotate(q_heads.reshape(count, heads_here, HD), cosine, sine)
    key_rot = rotate(k_heads.reshape(count, heads_here, HD), cosine, sine)
    mixed = attend(query_rot, key_rot, v_heads.reshape(count, heads_here, HD), length)
    mixed = mixed.reshape(count, 1, heads_here, HD)
    returned = lax.all_to_all(mixed, "seq", split_axis=0, concat_axis=1, tiled=True)
    returned = returned.reshape(tok_rows, feature_count).astype(jnp.float32)
    position = lax.axis_index("seq") * tok_rows + jnp.arange(tok_rows, dtype=jnp.int32)
    gated = returned * (1.0 + sigma * gate_gain[None, :])
    attended = jnp.where(position[:, None] < length, gated, 0.0).astype(jnp.bfloat16)
    return attended[None]


def solution(mesh):
    finer = Mesh(mesh.devices.reshape(4, 8, mesh.shape["seq"]), ("clip_0", "clip_1", "seq"))
    in_specs = (
        P(CLIP, "seq", None),
        P(CLIP, "seq", None),
        P(CLIP, "seq", None),
        P(CLIP),
        P(CLIP),
        P(CLIP),
        P(),
    )
    out_specs = P(CLIP, "seq", None)
    return jax.shard_map(local, mesh=finer, in_specs=in_specs, out_specs=out_specs, check_vma=False)
```

profile of v0, /device:TPU:1, one launch (start us, length us, event | category | flops | bytes accessed | tf_op | source)
XLA Modules:
  0.0 183.7 jit_solution(16581078526620594948)
XLA Ops:
  0.0 2.3 %copy.23 = bf16[1,128,4096]{1,2,0:T(8,128)(2,1)} copy(bf16[1,128,4096]{2,1,0:T(8,128)(2,1)} %param.7) | data formatting | bytes 2097152 | tf_op args[0]
  2.3 2.3 %copy.24 = bf16[1,128,4096]{1,2,0:T(8,128)(2,1)} copy(bf16[1,128,4096]{2,1,0:T(8,128)(2,1)} %param.8) | data formatting | bytes 2097152 | tf_op args[1]
  4.6 2.3 %copy.25 = bf16[1,128,4096]{1,2,0:T(8,128)(2,1)} copy(bf16[1,128,4096]{2,1,0:T(8,128)(2,1)} %param.9) | data formatting | bytes 2097152 | tf_op args[2]
  6.8 2.0 %pad_maximum_fusion = bf16[128,16,6,128]{0,3,2,1:T(8,128)(2,1)S(1)} fusion(bf16[128,16,2,128]{0,3,2,1:T(8,128)(2,1)} %bitcast.88, bf16[128,16,2,128]{0,3,2,1:T(8,128)(2,1)} %bitcast.87, bf16[128,16,2,128]{0,3,2,1:T(8,128)(2,1)} %bitcast.86), kind=kLoop, calls=%fused_computation.28 | loop fusion | flops 3145728 | bytes 6291456 | tf_op jit(solution)/shard_map/concatenate | solution.py:34
  8.9 2.8 %copy.26 = bf16[128,16,6,128]{3,0,2,1:T(8,128)(2,1)} copy(bf16[128,16,6,128]{0,3,2,1:T(8,128)(2,1)S(1)} %pad_maximum_fusion) | data formatting | bytes 6291456 | tf_op jit(solution)/shard_map/concatenate | solution.py:34
  11.7 11.8 %all-to-all-start = ((bf16[128,16,6,128]{3,0,2,1:T(8,128)(2,1)}), bf16[128,16,6,128]{3,0,2,1:T(8,128)(2,1)S(1)}, u32[]{:S(2)}, u32[]{:S(2)}) async-start(bf16[128,16,6,128]{3,0,2,1:T(8,128)(2,1)} %copy.26), calls=%async_computation | async-start | bytes 6291456 | tf_op jit(solution)/shard_map/all_to_all | solution.py:36
  23.5 1.3 dynamic-slice
  25.7 7.4 %all-reduce = s32[16]{0:T(128)S(1)} all-reduce(s32[16]{0:T(128)S(1)} %dynamic-update-slice), channel_id=2, replica_groups=mesh['clip_0'=4,'clip_1'=8,'seq'=16] {'clip_0'}, use_global_device_ids=true, to_apply=%add | all-reduce | flops 16 | bytes 128
  33.9 20.1 %all-gather.2 = s32[8,4,4]{2,1,0:T(4,128)S(1)} all-gather(s32[1,4,4]{2,1,0:T(4,128)S(1)} %reshape.313), channel_id=3, replica_groups=mesh['clip_0'=4,'clip_1'=8,'seq'=16] {'clip_1'}, dimensions={0}, use_global_device_ids=true | all-gather | bytes 576 | tf_op jit(solution)/shard_map/all_gather | solution.py:22
  53.9 0.6 fusion.91
  55.5 0.6 broadcast_multiply_fusion.1
  56.1 5.2 %fusion.123 = (f32[2048,64]{1,0:T(8,128)}, f32[2048,64]{1,0:T(8,128)}) fusion(f32[2048,21]{1,0:T(8,128)S(1)} %get-tuple-element.23, f32[2048,21]{1,0:T(8,128)S(1)} %get-tuple-element.22, f32[2048,22]{1,0:T(8,128)S(1)} %broadcast_multiply_fusion.2), kind=kLoop, calls=%fused_computation.132 | loop fusion | flops 262144 | bytes 1572864 | tf_op jit(solution)/shard_map/cos | solution.py:64
  61.3 33.2 %all-to-all-done = bf16[128,16,6,128]{3,0,2,1:T(8,128)(2,1)S(1)} async-done(((bf16[128,16,6,128]{3,0,2,1:T(8,128)(2,1)}), bf16[128,16,6,128]{3,0,2,1:T(8,128)(2,1)S(1)}, u32[]{:S(2)}, u32[]{:S(2)}) %all-to-all-start) | async-done | bytes 3145760 | tf_op jit(solution)/shard_map/all_to_all | solution.py:36
  94.9 1.0 copy-done.4
  95.9 1.1 copy-done.5
  97.0 1.8 fusion.25
  99.4 1.3 fusion.81
  100.7 1.3 fusion.89
  102.0 4.6 %fusion = (f32[2,512]{1,0:T(2,128)S(1)}, f32[2,512,2048]{2,1,0:T(8,128)}) fusion(pred[2048]{0:T(1024)(128)(4,1)S(1)} %iota_compare_fusion, bf16[2048,2,128]{2,0,1:T(8,128)(2,1)S(1)} %pad_maximum_fusion.2, bf16[2048,2,64]{2,0,1:T(8,128)(2,1)S(1)} %get-tuple-element.12, bf16[2048,2,64]{2,0,1:T(8,128)(2,1)S(1)} %get-tuple-element.13), kind=kOutput, calls=%fused_computation.8 | convolution fusion | flops 543685632 | bytes 10491904 | tf_op jit(solution)/shard_map/qhd,khd->hqk/dot_general | solution.py:80
  106.6 10.3 %fusion.4 = (f32[2,512]{1,0:T(2,128)}, f32[2,512]{1,0:T(2,128)}, f32[2,512]{1,0:T(2,128)}, f32[2,512]{1,0:T(2,128)S(1)}, f32[2,512,2048]{2,1,0:T(8,128)}) fusion(f32[2,512,2048]{2,1,0:T(8,128)} %get-tuple-element.25, f32[2,512]{1,0:T(2,128)S(1)} %get-tuple-element.24, pred[2048]{0:T(1024)(128)(4,1)S(1)} %iota_compare_fusion, ...), kind=kOutput, calls=%fused_computation.12 | convolution fusion | flops 564654080 | bytes 35674112 | tf_op jit(solution)/shard_map/qhd,khd->hqk/dot_general | solution.py:80
  116.9 5.7 %fusion.77 = bf16[512,1,2,128]{0,3,2,1:T(8,128)(2,1)S(1)} fusion(f32[2,512,2048]{2,1,0:T(8,128)} %get-tuple-element.25, f32[2,512]{1,0:T(2,128)S(1)} %get-tuple-element.24, pred[2048]{0:T(1024)(128)(4,1)S(1)} %iota_compare_fusion, bf16[2048,1,6,128]{3,0,2,1:T(8,128)(2,1)} %bitcast.81, f32[512,2]{0,1:T(2,128)} %bitcast.92), kind=kOutput, calls=%fused_computation.68 | convolution fusion | flops 545521664 | bytes 9709568 | tf_op jit(solution)/shard_map/hqk,khd->qhd/dot_general | solution.py:97
  122.6 7.8 %fusion.6 = (f32[2,512]{1,0:T(2,128)S(1)}, f32[2,512]{1,0:T(2,128)S(1)}, f32[2,512]{1,0:T(2,128)S(1)}) fusion(f32[2,512,2048]{2,1,0:T(8,128)} %get-tuple-element.26, f32[2,512]{1,0:T(2,128)S(1)} %copy-done.8, pred[2048]{0:T(1024)(128)(4,1)S(1)} %iota_compare_fusion, f32[2,512]{1,0:T(2,128)S(1)} %copy-done.7, f32[2,512,2048]{2,1,0:T(8,128)S(1)} %fusion.81, ...), kind=kLoop, calls=%fused_computation.14 | loop fusion | flops 25162752 | bytes 25192448 | tf_op jit(solution)/shard_map/reduce_sum | solution.py:96
  130.4 5.4 %fusion.68 = bf16[512,1,2,128]{0,3,2,1:T(8,128)(2,1)S(1)} fusion(f32[2,512,2048]{2,1,0:T(8,128)} %get-tuple-element.26, f32[2,512]{1,0:T(2,128)S(1)} %copy-done.8, pred[2048]{0:T(1024)(128)(4,1)S(1)} %iota_compare_fusion, bf16[2048,1,6,128]{3,0,2,1:T(8,128)(2,1)S(1)} %bitcast.82, f32[512,2]{0,1:T(2,128)S(1)} %bitcast.91), kind=kOutput, calls=%fused_computation.65 | convolution fusion | flops 545521664 | bytes 9709568 | tf_op jit(solution)/shard_map/hqk,khd->qhd/dot_general | solution.py:97
  135.8 2.3 %fusion.59 = bf16[512,1,2,128]{0,3,2,1:T(8,128)(2,1)S(1)} fusion(f32[2,512,2048]{2,1,0:T(8,128)S(1)} %fusion.81, f32[2,512]{1,0:T(2,128)S(1)} %copy-done.7, pred[2048]{0:T(1024)(128)(4,1)S(1)} %iota_compare_fusion, bf16[2048,1,6,128]{3,0,2,1:T(8,128)(2,1)S(1)} %bitcast.83, f32[512,2]{0,1:T(2,128)S(1)} %bitcast.90), kind=kOutput, calls=%fused_computation.62 | convolution fusion | flops 545521664 | bytes 9709568 | tf_op jit(solution)/shard_map/hqk,khd->qhd/dot_general | solution.py:97
  138.2 2.4 %fusion.50 = bf16[512,1,2,128]{0,3,2,1:T(8,128)(2,1)S(1)} fusion(f32[2,512,2048]{2,1,0:T(8,128)S(1)} %fusion.89, f32[2,512]{1,0:T(2,128)S(1)} %get-tuple-element.8, pred[2048]{0:T(1024)(128)(4,1)S(1)} %iota_compare_fusion, bf16[2048,1,6,128]{3,0,2,1:T(8,128)(2,1)S(1)} %bitcast.84, f32[512,2]{0,1:T(2,128)S(1)} %bitcast.89), kind=kOutput, calls=%fused_computation.59 | convolution fusion | flops 545521664 | bytes 9709568 | tf_op jit(solution)/shard_map/hqk,khd->qhd/dot_general | solution.py:97
  140.7 2.0 %copy.32 = bf16[2048,1,2,128]{3,2,1,0:T(2,128)(2,1)} copy(bf16[2048,1,2,128]{0,3,2,1:T(8,128)(2,1)S(1)} %pad_maximum_fusion.3) | data formatting | bytes 2097152 | tf_op jit(solution)/shard_map/concatenate | solution.py:101
  142.7 5.4 %all-to-all-start.1 = ((bf16[2048,1,2,128]{3,2,1,0:T(2,128)(2,1)}), bf16[2048,1,2,128]{3,2,1,0:T(2,128)(2,1)S(1)}, u32[]{:S(2)}, u32[]{:S(2)}) async-start(bf16[2048,1,2,128]{3,2,1,0:T(2,128)(2,1)} %copy.32), calls=%async_computation.1 | async-start | bytes 2097152 | tf_op jit(solution)/shard_map/all_to_all | solution.py:126
  148.9 27.2 %all-to-all-done.1 = bf16[2048,1,2,128]{3,2,1,0:T(2,128)(2,1)S(1)} async-done(((bf16[2048,1,2,128]{3,2,1,0:T(2,128)(2,1)}), bf16[2048,1,2,128]{3,2,1,0:T(2,128)(2,1)S(1)}, u32[]{:S(2)}, u32[]{:S(2)}) %all-to-all-start.1) | async-done | bytes 1048608 | tf_op jit(solution)/shard_map/all_to_all | solution.py:126
  176.1 0.9 convert_bitcast_fusion
  177.0 2.6 %copy.33 = f32[128,16,1,2,128]{4,3,1,0,2:T(2,128)} copy(f32[128,16,1,2,128]{4,3,0,1,2:T(2,128)S(1)} %convert_bitcast_fusion) | data formatting | bytes 4194304 | tf_op jit(solution)/shard_map/convert_element_type | solution.py:127
  179.5 2.9 %reshape.306 = f32[1,128,4096]{2,1,0:T(8,128)S(1)} reshape(f32[128,16,1,2,128]{4,3,1,0,2:T(2,128)} %copy.33) | data formatting | bytes 4194304 | tf_op jit(solution)/shard_map/convert_element_type | solution.py:127
  182.5 1.2 select_convert_fusion
  (33 shorter events, 1.9 us)
Async XLA Ops:
  6.8 18.6 %copy-start.9 = (s32[4]{0:T(128)S(1)}, s32[4]{0:T(128)}, u32[]{:S(2)}) copy-start(s32[4]{0:T(128)} %param.10) | copy-start | bytes 52
  11.7 82.8 %all-to-all-start = ((bf16[128,16,6,128]{3,0,2,1:T(8,128)(2,1)}), bf16[128,16,6,128]{3,0,2,1:T(8,128)(2,1)S(1)}, u32[]{:S(2)}, u32[]{:S(2)}) async-start(bf16[128,16,6,128]{3,0,2,1:T(8,128)(2,1)} %copy.26), calls=%async_computation | async-start | bytes 6291456 | tf_op jit(solution)/shard_map/all_to_all | solution.py:36
  94.5 1.4 copy-start.4
  94.5 2.5 %copy-start.5 = (f32[2048,64]{1,0:T(8,128)S(1)}, f32[2048,64]{1,0:T(8,128)}, u32[]{:S(2)}) copy-start(f32[2048,64]{1,0:T(8,128)} %get-tuple-element.19) | copy-start | bytes 1572868
  94.7 4.7 %copy-start.2 = (bf16[16,128,1,6,128]{4,1,0,3,2:T(8,128)(2,1)}, bf16[16,128,1,6,128]{4,1,0,3,2:T(8,128)(2,1)S(1)}, u32[]{:S(2)}) copy-start(bf16[16,128,1,6,128]{4,1,0,3,2:T(8,128)(2,1)S(1)} %copy.27) | copy-start | bytes 9437188
  98.8 3.2 %copy-start = (bf16[2048,2,64]{2,0,1:T(8,128)(2,1)}, bf16[2048,2,64]{2,0,1:T(8,128)(2,1)S(1)}, u32[]{:S(2)}) copy-start(bf16[2048,2,64]{2,0,1:T(8,128)(2,1)S(1)} %get-tuple-element.13) | copy-start | bytes 1572868
  99.4 2.6 %copy-start.1 = (bf16[2048,2,128]{2,0,1:T(8,128)(2,1)}, bf16[2048,2,128]{2,0,1:T(8,128)(2,1)S(1)}, u32[]{:S(2)}) copy-start(bf16[2048,2,128]{2,0,1:T(8,128)(2,1)S(1)} %pad_maximum_fusion.2) | copy-start | bytes 3145732
  116.9 5.7 %copy-start.7 = (f32[2,512]{1,0:T(2,128)S(1)}, f32[2,512]{1,0:T(2,128)}, u32[]{:S(2)}) copy-start(f32[2,512]{1,0:T(2,128)} %get-tuple-element.7) | copy-start | bytes 12292
  116.9 5.7 %copy-start.8 = (f32[2,512]{1,0:T(2,128)S(1)}, f32[2,512]{1,0:T(2,128)}, u32[]{:S(2)}) copy-start(f32[2,512]{1,0:T(2,128)} %get-tuple-element.6) | copy-start | bytes 12292
  122.6 7.8 %copy-start.3 = (bf16[16,128,1,6,128]{4,1,0,3,2:T(8,128)(2,1)S(1)}, bf16[16,128,1,6,128]{4,1,0,3,2:T(8,128)(2,1)}, u32[]{:S(2)}) copy-start(bf16[16,128,1,6,128]{4,1,0,3,2:T(8,128)(2,1)} %copy-done.2) | copy-start | bytes 9437188
  138.2 10.7 %copy-start.6 = (f32[4096]{0:T(1024)S(1)}, f32[4096]{0:T(1024)}, u32[]{:S(2)}) copy-start(f32[4096]{0:T(1024)} %param.13) | copy-start | bytes 49156
  142.7 33.4 %all-to-all-start.1 = ((bf16[2048,1,2,128]{3,2,1,0:T(2,128)(2,1)}), bf16[2048,1,2,128]{3,2,1,0:T(2,128)(2,1)S(1)}, u32[]{:S(2)}, u32[]{:S(2)}) async-start(bf16[2048,1,2,128]{3,2,1,0:T(2,128)(2,1)} %copy.32), calls=%async_computation.1 | async-start | bytes 2097152 | tf_op jit(solution)/shard_map/all_to_all | solution.py:126
where the time goes:
time: 184 us
  waiting for transfers between devices  60.4 us (33%)
  matrix products  33.3 us (18%)
  blocking collectives  27.5 us (15%)
  local copies, waits for them, and re-layouts  21.2 us (12%)
  other arithmetic  21.2 us (12%)
  starting transfers between devices  17.3 us (9%)
  between operations  2.83 us (2%)
    all_to_all x1, waiting for transfers between devices, sent_together(): lax.all_to_all(both, axis, split_axis=split_dim, concat_axis=concat_dim,...  33.2 us
    all_to_all x1, waiting for transfers between devices, local(): lax.all_to_all(mixed, 'seq', split_axis=0, concat_axis=1, tiled=True)  27.2 us
    all_gather x1, blocking collectives, all_blocks(): tiles = lax.all_gather(tiles, axes[k])  20.1 us
    dot_general x4, matrix products, masked_scores(): jnp.einsum('qhd,khd->hqk', q_block, key_rot, preferred_element_type=jnp.f...  17.4 us
    dot_general x4, matrix products, attend(): jnp.einsum('hqk,khd->qhd', weights.astype(jnp.bfloat16), value, preferred...  15.8 us
    all_to_all x1, starting transfers between devices, sent_together(): lax.all_to_all(both, axis, split_axis=split_dim, concat_axis=concat_dim,...  11.8 us
    unnamed x27, local copies, waits for them, and re-layouts  10.6 us
    reduce_sum x1, other arithmetic, attend(): total = jnp.sum(weights, axis=-1)  7.78 us
  transfers between devices with their start and end apart: 2, of which 2 were waited for; matrix products, arithmetic and copies ran while one was open for 5% of the time, Pallas kernels for 0%

commit v1 on v0

--- a/solution.py
+++ b/solution.py
@@ -123,7 +123,10 @@
     key_rot = rotate(k_heads.reshape(count, heads_here, HD), cosine, sine)
     mixed = attend(query_rot, key_rot, v_heads.reshape(count, heads_here, HD), length)
     mixed = mixed.reshape(count, 1, heads_here, HD)
-    returned = lax.all_to_all(mixed, "seq", split_axis=0, concat_axis=1, tiled=True)
+    returned = jnp.concatenate(
+        lax.all_to_all(jnp.stack(jnp.split(mixed, lax.axis_size("seq"), axis=0)), "seq", 0, 0),
+        axis=1,
+    )
     returned = returned.reshape(tok_rows, feature_count).astype(jnp.float32)
     position = lax.axis_index("seq") * tok_rows + jnp.arange(tok_rows, dtype=jnp.int32)
     gated = returned * (1.0 + sigma * gate_gain[None, :])

time: 184 us -> 184 us (level)
  local copies, waits for them, and re-layouts: 21.2 us -> 26.1 us
  other arithmetic: 21.2 us -> 17.7 us
    unnamed x27 -> x44, local copies, waits for them, and re-layouts: 10.6 us -> 20.4 us
    reduce_sum x1, other arithmetic: 7.78 us -> 3.69 us  [attend(): total = jnp.sum(weights, axis=-1)]
    convert_element_type x2 -> x1, local copies, waits for them, and re-layouts: 5.48 us -> 1.92 us  [local(): returned = returned.reshape(tok_rows, feature_count).astype(jnp.float32)]
    dot_general x4, matrix products: 15.8 us -> 12.9 us  [attend(): jnp.einsum('hqk,khd->qhd', weights.astype(jnp.bfloat16), value, preferred...]
    concatenate x1 -> x0, local copies, waits for them, and re-layouts: 2 us -> none  [attend(): return jnp.concatenate(results, axis=0).astype(jnp.bfloat16)]
where the time goes in v1:
time: 184 us; the launch traced here: 183 us
  waiting for transfers between devices  60.4 us (33%)
  matrix products  31.5 us (17%)
  blocking collectives  27.5 us (15%)
  local copies, waits for them, and re-layouts  26.1 us (14%)
  other arithmetic  17.7 us (10%)
  starting transfers between devices  17.3 us (9%)
  between operations  2.81 us (2%)
    all_to_all x1, waiting for transfers between devices, sent_together(): lax.all_to_all(both, axis, split_axis=split_dim, concat_axis=concat_dim,...  33.2 us
    all_to_all x1, waiting for transfers between devices, local(): lax.all_to_all(jnp.stack(jnp.split(mixed, lax.axis_size('seq'), axis=0)),...  27.2 us
    unnamed x44, local copies, waits for them, and re-layouts  20.4 us
    all_gather x1, blocking collectives, all_blocks(): tiles = lax.all_gather(tiles, axes[k])  20.1 us
    dot_general x4, matrix products, masked_scores(): jnp.einsum('qhd,khd->hqk', q_block, key_rot, preferred_element_type=jnp.f...  18.7 us
    dot_general x4, matrix products, attend(): jnp.einsum('hqk,khd->qhd', weights.astype(jnp.bfloat16), value, preferred...  12.9 us
    all_to_all x1, starting transfers between devices, sent_together(): lax.all_to_all(both, axis, split_axis=split_dim, concat_axis=concat_dim,...  11.8 us
    unnamed x1, blocking collectives  7.45 us
  transfers between devices with their start and end apart: 2, of which 2 were waited for; matrix products, arithmetic and copies ran while one was open for 5% of the time, Pallas kernels for 0%

profile of v1, /device:TPU:1, one launch (start us, length us, event | category | flops | bytes accessed | tf_op | source)
XLA Modules:
  0.0 183.3 jit_solution(6014155866692101332)
XLA Ops:
  0.0 2.3 %copy.22 = bf16[1,128,4096]{1,2,0:T(8,128)(2,1)} copy(bf16[1,128,4096]{2,1,0:T(8,128)(2,1)} %param.7) | data formatting | bytes 2097152 | tf_op args[0]
  2.3 2.3 %copy.23 = bf16[1,128,4096]{1,2,0:T(8,128)(2,1)} copy(bf16[1,128,4096]{2,1,0:T(8,128)(2,1)} %param.8) | data formatting | bytes 2097152 | tf_op args[1]
  4.6 2.3 %copy.24 = bf16[1,128,4096]{1,2,0:T(8,128)(2,1)} copy(bf16[1,128,4096]{2,1,0:T(8,128)(2,1)} %param.9) | data formatting | bytes 2097152 | tf_op args[2]
  6.8 2.0 %pad_maximum_fusion = bf16[128,16,6,128]{0,3,2,1:T(8,128)(2,1)S(1)} fusion(bf16[128,16,2,128]{0,3,2,1:T(8,128)(2,1)} %bitcast.133, bf16[128,16,2,128]{0,3,2,1:T(8,128)(2,1)} %bitcast.132, bf16[128,16,2,128]{0,3,2,1:T(8,128)(2,1)} %bitcast.131), kind=kLoop, calls=%fused_computation.28 | loop fusion | flops 3145728 | bytes 6291456 | tf_op jit(solution)/shard_map/concatenate | solution.py:34
  8.9 2.8 %copy.25 = bf16[128,16,6,128]{3,0,2,1:T(8,128)(2,1)} copy(bf16[128,16,6,128]{0,3,2,1:T(8,128)(2,1)S(1)} %pad_maximum_fusion) | data formatting | bytes 6291456 | tf_op jit(solution)/shard_map/concatenate | solution.py:34
  11.7 11.8 %all-to-all-start = ((bf16[128,16,6,128]{3,0,2,1:T(8,128)(2,1)}), bf16[128,16,6,128]{3,0,2,1:T(8,128)(2,1)S(1)}, u32[]{:S(2)}, u32[]{:S(2)}) async-start(bf16[128,16,6,128]{3,0,2,1:T(8,128)(2,1)} %copy.25), calls=%async_computation | async-start | bytes 6291456 | tf_op jit(solution)/shard_map/all_to_all | solution.py:36
  23.5 1.3 dynamic-slice
  25.7 7.4 %all-reduce = s32[16]{0:T(128)S(1)} all-reduce(s32[16]{0:T(128)S(1)} %dynamic-update-slice), channel_id=2, replica_groups=mesh['clip_0'=4,'clip_1'=8,'seq'=16] {'clip_0'}, use_global_device_ids=true, to_apply=%add | all-reduce | flops 16 | bytes 128
  33.9 20.1 %all-gather.2 = s32[8,4,4]{2,1,0:T(4,128)S(1)} all-gather(s32[1,4,4]{2,1,0:T(4,128)S(1)} %reshape.282), channel_id=3, replica_groups=mesh['clip_0'=4,'clip_1'=8,'seq'=16] {'clip_1'}, dimensions={0}, use_global_device_ids=true | all-gather | bytes 576 | tf_op jit(solution)/shard_map/all_gather | solution.py:22
  56.1 5.2 %fusion.127 = (f32[2048,64]{1,0:T(8,128)}, f32[2048,64]{1,0:T(8,128)}) fusion(f32[2048,21]{1,0:T(8,128)S(1)} %get-tuple-element.24, f32[2048,21]{1,0:T(8,128)S(1)} %get-tuple-element.23, f32[2048,22]{1,0:T(8,128)S(1)} %broadcast_multiply_fusion.2), kind=kLoop, calls=%fused_computation.158 | loop fusion | flops 262144 | bytes 1572864 | tf_op jit(solution)/shard_map/cos | solution.py:64
  61.3 33.2 %all-to-all-done = bf16[128,16,6,128]{3,0,2,1:T(8,128)(2,1)S(1)} async-done(((bf16[128,16,6,128]{3,0,2,1:T(8,128)(2,1)}), bf16[128,16,6,128]{3,0,2,1:T(8,128)(2,1)S(1)}, u32[]{:S(2)}, u32[]{:S(2)}) %all-to-all-start) | async-done | bytes 3145760 | tf_op jit(solution)/shard_map/all_to_all | solution.py:36
  94.9 1.0 copy-done.5
  95.9 1.1 copy-done.6
  97.0 1.8 fusion.27
  99.4 1.3 fusion.72
  100.7 1.3 fusion.69
  102.0 5.0 %fusion.3 = (f32[2,512]{1,0:T(2,128)}, f32[2,512]{1,0:T(2,128)S(1)}, f32[2,512,2048]{2,1,0:T(8,128)}) fusion(pred[2048]{0:T(1024)(128)(4,1)S(1)} %iota_compare_fusion, f32[2,512,2048]{2,1,0:T(8,128)S(1)} %fusion.72, bf16[2048,2,128]{2,0,1:T(8,128)(2,1)S(1)} %pad_maximum_fusion.2, bf16[2048,2,64]{2,0,1:T(8,128)(2,1)S(1)} %get-tuple-element.13, ...), kind=kOutput, calls=%fused_computation.11 | convolution fusion | flops 549976064 | bytes 18884608 | tf_op jit(solution)/shard_map/qhd,khd->hqk/dot_general | solution.py:80
  107.1 11.0 %fusion.10 = (f32[2,512]{1,0:T(2,128)}, f32[2,512]{1,0:T(2,128)S(1)}, f32[2,512]{1,0:T(2,128)}, f32[2,512]{1,0:T(2,128)}, f32[2,512,2048]{2,1,0:T(8,128)}) fusion(f32[2,512,2048]{2,1,0:T(8,128)} %get-tuple-element.25, f32[2,512]{1,0:T(2,128)} %get-tuple-element.9, pred[2048]{0:T(1024)(128)(4,1)S(1)} %iota_compare_fusion, f32[2,512,2048]{2,1,0:T(8,128)S(1)} %fusion.69, ...), kind=kOutput, calls=%fused_computation.18 | convolution fusion | flops 566751232 | bytes 35678208 | tf_op jit(solution)/shard_map/qhd,khd->hqk/dot_general | solution.py:80
  118.1 5.8 %fusion.47 = bf16[512,2,128]{0,2,1:T(8,128)(2,1)S(1)} fusion(f32[2,512,2048]{2,1,0:T(8,128)} %get-tuple-element.25, f32[2,512]{1,0:T(2,128)} %get-tuple-element.9, pred[2048]{0:T(1024)(128)(4,1)S(1)} %iota_compare_fusion, bf16[2048,1,6,128]{3,0,2,1:T(8,128)(2,1)} %bitcast.126, f32[512,2]{0,1:T(2,128)} %bitcast.137), kind=kOutput, calls=%fused_computation.56 | convolution fusion | flops 545521664 | bytes 9709568 | tf_op jit(solution)/shard_map/hqk,khd->qhd/dot_general | solution.py:97
  124.2 3.7 %fusion.8 = (f32[2,512]{1,0:T(2,128)S(1)}, f32[2,512]{1,0:T(2,128)S(1)}) fusion(f32[2,512,2048]{2,1,0:T(8,128)S(1)} %fusion.69, f32[2,512]{1,0:T(2,128)S(1)} %copy-done.8, pred[2048]{0:T(1024)(128)(4,1)S(1)} %iota_compare_fusion, f32[2,512]{1,0:T(2,128)S(1)} %get-tuple-element.6, f32[2,512,2048]{2,1,0:T(8,128)S(1)} %copy-done.4), kind=kLoop, calls=%fused_computation.16 | loop fusion | flops 16775168 | bytes 16795648 | tf_op jit(solution)/shard_map/reduce_sum | solution.py:96
  127.9 2.3 %fusion.53 = bf16[512,2,128]{0,2,1:T(8,128)(2,1)S(1)} fusion(f32[2,512,2048]{2,1,0:T(8,128)S(1)} %fusion.69, f32[2,512]{1,0:T(2,128)S(1)} %copy-done.8, pred[2048]{0:T(1024)(128)(4,1)S(1)} %iota_compare_fusion, bf16[2048,1,6,128]{3,0,2,1:T(8,128)(2,1)S(1)} %bitcast.127, f32[512,2]{0,1:T(2,128)S(1)} %bitcast.135), kind=kOutput, calls=%fused_computation.58 | convolution fusion | flops 545521664 | bytes 9709568 | tf_op jit(solution)/shard_map/hqk,khd->qhd/dot_general | solution.py:97
  130.3 2.3 %fusion.59 = bf16[512,2,128]{0,2,1:T(8,128)(2,1)S(1)} fusion(f32[2,512,2048]{2,1,0:T(8,128)S(1)} %copy-done.4, f32[2,512]{1,0:T(2,128)S(1)} %get-tuple-element.6, pred[2048]{0:T(1024)(128)(4,1)S(1)} %iota_compare_fusion, bf16[2048,1,6,128]{3,0,2,1:T(8,128)(2,1)S(1)} %bitcast.128, f32[512,2]{0,1:T(2,128)S(1)} %bitcast.134), kind=kOutput, calls=%fused_computation.60 | convolution fusion | flops 545521664 | bytes 9709568 | tf_op jit(solution)/shard_map/hqk,khd->qhd/dot_general | solution.py:97
  132.6 2.4 %fusion.65 = bf16[512,2,128]{0,2,1:T(8,128)(2,1)S(1)} fusion(f32[2,512,2048]{2,1,0:T(8,128)S(1)} %fusion.72, f32[2,512]{1,0:T(2,128)S(1)} %get-tuple-element.10, pred[2048]{0:T(1024)(128)(4,1)S(1)} %iota_compare_fusion, bf16[2048,1,6,128]{3,0,2,1:T(8,128)(2,1)S(1)} %bitcast.129, f32[512,2]{0,1:T(2,128)S(1)} %bitcast.136), kind=kOutput, calls=%fused_computation.62 | convolution fusion | flops 545521664 | bytes 9709568 | tf_op jit(solution)/shard_map/hqk,khd->qhd/dot_general | solution.py:97
  135.0 0.6 fusion.94
  135.6 0.6 fusion.93
  136.3 0.6 fusion.92
  136.9 0.6 fusion.91
  145.2 5.4 %all-to-all-start.1 = ((bf16[16,128,1,2,128]{1,4,3,2,0:T(8,128)(2,1)}), bf16[16,128,1,2,128]{1,4,3,2,0:T(8,128)(2,1)S(1)}, u32[]{:S(2)}, u32[]{:S(2)}) async-start(bf16[16,128,1,2,128]{1,4,3,2,0:T(8,128)(2,1)} %fusion.79), calls=%async_computation.1 | async-start | bytes 2097152 | tf_op jit(solution)/shard_map/all_to_all | solution.py:127
  151.4 27.2 %all-to-all-done.1 = bf16[16,128,1,2,128]{1,4,3,2,0:T(8,128)(2,1)S(1)} async-done(((bf16[16,128,1,2,128]{1,4,3,2,0:T(8,128)(2,1)}), bf16[16,128,1,2,128]{1,4,3,2,0:T(8,128)(2,1)S(1)}, u32[]{:S(2)}, u32[]{:S(2)}) %all-to-all-start.1) | async-done | bytes 1048608 | tf_op jit(solution)/shard_map/all_to_all | solution.py:127
  178.6 1.6 convert_element_type.95
  180.2 1.9 %copy.31 = f32[1,128,4096]{2,1,0:T(8,128)S(1)} copy(f32[1,128,4096]{1,2,0:T(8,128)} %bitcast.130) | data formatting | bytes 4194304 | tf_op jit(solution)/shard_map/convert_element_type | solution.py:130
  182.1 1.2 select_convert_fusion
  (48 shorter events, 10.8 us)
Async XLA Ops:
  6.8 18.6 %copy-start.9 = (s32[4]{0:T(128)S(1)}, s32[4]{0:T(128)}, u32[]{:S(2)}) copy-start(s32[4]{0:T(128)} %param.10) | copy-start | bytes 52
  11.7 82.8 %all-to-all-start = ((bf16[128,16,6,128]{3,0,2,1:T(8,128)(2,1)}), bf16[128,16,6,128]{3,0,2,1:T(8,128)(2,1)S(1)}, u32[]{:S(2)}, u32[]{:S(2)}) async-start(bf16[128,16,6,128]{3,0,2,1:T(8,128)(2,1)} %copy.25), calls=%async_computation | async-start | bytes 6291456 | tf_op jit(solution)/shard_map/all_to_all | solution.py:36
  94.5 1.4 copy-start.5
  94.5 2.5 %copy-start.6 = (f32[2048,64]{1,0:T(8,128)S(1)}, f32[2048,64]{1,0:T(8,128)}, u32[]{:S(2)}) copy-start(f32[2048,64]{1,0:T(8,128)} %get-tuple-element.20) | copy-start | bytes 1572868
  94.7 4.7 %copy-start.2 = (bf16[16,128,1,6,128]{4,1,0,3,2:T(8,128)(2,1)}, bf16[16,128,1,6,128]{4,1,0,3,2:T(8,128)(2,1)S(1)}, u32[]{:S(2)}) copy-start(bf16[16,128,1,6,128]{4,1,0,3,2:T(8,128)(2,1)S(1)} %copy.26) | copy-start | bytes 9437188
  98.8 3.2 %copy-start = (bf16[2048,2,64]{2,0,1:T(8,128)(2,1)}, bf16[2048,2,64]{2,0,1:T(8,128)(2,1)S(1)}, u32[]{:S(2)}) copy-start(bf16[2048,2,64]{2,0,1:T(8,128)(2,1)S(1)} %get-tuple-element.14) | copy-start | bytes 1572868
  99.4 2.6 %copy-start.1 = (bf16[2048,2,128]{2,0,1:T(8,128)(2,1)}, bf16[2048,2,128]{2,0,1:T(8,128)(2,1)S(1)}, u32[]{:S(2)}) copy-start(bf16[2048,2,128]{2,0,1:T(8,128)(2,1)S(1)} %pad_maximum_fusion.2) | copy-start | bytes 3145732
  118.1 6.1 %copy-start.4 = (f32[2,512,2048]{2,1,0:T(8,128)S(1)}, f32[2,512,2048]{2,1,0:T(8,128)}, u32[]{:S(2)}) copy-start(f32[2,512,2048]{2,1,0:T(8,128)} %get-tuple-element.26) | copy-start | bytes 25165828
  118.1 6.1 %copy-start.8 = (f32[2,512]{1,0:T(2,128)S(1)}, f32[2,512]{1,0:T(2,128)}, u32[]{:S(2)}) copy-start(f32[2,512]{1,0:T(2,128)} %get-tuple-element.7) | copy-start | bytes 12292
  124.2 3.7 %copy-start.3 = (bf16[16,128,1,6,128]{4,1,0,3,2:T(8,128)(2,1)S(1)}, bf16[16,128,1,6,128]{4,1,0,3,2:T(8,128)(2,1)}, u32[]{:S(2)}) copy-start(bf16[16,128,1,6,128]{4,1,0,3,2:T(8,128)(2,1)} %copy-done.2) | copy-start | bytes 9437188
  130.2 2.4 %copy-start.10 = (f32[2,512]{1,0:T(2,128)S(1)}, f32[2,512]{1,0:T(2,128)}, u32[]{:S(2)}) copy-start(f32[2,512]{1,0:T(2,128)} %get-tuple-element.8) | copy-start | bytes 12292
  132.6 18.7 %copy-start.7 = (f32[4096]{0:T(1024)S(1)}, f32[4096]{0:T(1024)}, u32[]{:S(2)}) copy-start(f32[4096]{0:T(1024)} %param.13) | copy-start | bytes 49156
  145.2 33.4 %all-to-all-start.1 = ((bf16[16,128,1,2,128]{1,4,3,2,0:T(8,128)(2,1)}), bf16[16,128,1,2,128]{1,4,3,2,0:T(8,128)(2,1)S(1)}, u32[]{:S(2)}, u32[]{:S(2)}) async-start(bf16[16,128,1,2,128]{1,4,3,2,0:T(8,128)(2,1)} %fusion.79), calls=%async_computation.1 | async-start | bytes 2097152 | tf_op jit(solution)/shard_map/all_to_all | solution.py:127
